TPU v7x, 32 devices: a whole 2x2x4 slice. The times are simulated.
32 devices in a mesh: rows: 4 (over y, x), cols: 8 (over z, core).
Axes of the slice: x: 2, y: 2, z: 4, core: 2. Of those that a mesh axis runs over, the one named last changes fastest.
Arguments:
- c_eta: float32 [512, 2048], P('rows', 'cols'), may hold values from -4 to 4
- c_flux: float32 [2, 512, 2048], P(None, 'rows', 'cols'), may hold values from -150 to 150
- c_depth: float32 [512, 2048], P('rows', 'cols'), may hold values from 100 to 4000
- f_bed: float32 [128, 2048], P('rows', 'cols'), may hold values from -3 to 1
- f_depth: float32 [128, 2048], P('rows', 'cols'), may hold values from 0.05 to 3
- f_wet: int32 [128, 2048], P('rows', 'cols'), may hold values 0 or 1
- f_class: int32 [128, 2048], P('rows', 'cols'), may hold values from 0 to 10
- manning: float32 [11], replicated, may hold values from 0.02 to 0.2
- nest_map: int32 [2048], replicated, may hold values from 0 to 1048575, as said below
Outputs:
- c_eta_out: float32 [512, 2048], P('rows', 'cols')
- f_water: float32 [128, 2048], P('rows', 'cols')
- f_flux: float32 [2, 128, 2048], P(None, 'rows', 'cols')
Inputs may be any that keep to these rules, and one draw needn't show every extreme that they name: `nest_map`: entry b is the flat index, row times 2048 plus column, of the coarse cell that drives fine boundary cell b; entries with the same b // 18 are equal; for s = b // 18 the coarse row lies in [(s * 128) % 512, (s * 128) % 512 + 128) and the coarse column is min(s * 18 * 1 + 256 + j, 2047) for some j in 0..128.
All inputs are finite; a program needn't handle non-finite values. No bound on the sum of `f_wet` on one device may be relied on, other than what follows from the above.
Results may differ from a plain program's by a relative error of at most 0.00002.
Values sent between devices are 32-bit elements; how exact they have to be, the bound alone decides.
A program may use at most 64 MiB of HBM per device.

v0:
```python
import jax
import jax.numpy as jnp
from jax import lax
from jax.sharding import PartitionSpec as P

NCLASS = 11
CSTEPS = 2
SUB = 3
FSTEPS = 6
gravity = 9.81
coarse_spacing = 90.0
coarse_tick = 0.25
fine_spacing = 5.0
depth_floor = 0.01
dry_depth = 0.05


def padded_2(block, sides, width):
    for axis, dim in sides:
        count = lax.axis_size(axis)
        forward = [(i, i + 1) for i in range(count - 1)]
        backward = [(target, source) for source, target in forward]
        low = lax.ppermute(
            lax.slice_in_dim(block, block.shape[dim] - width, None, axis=dim), axis, forward
        )
        high = lax.ppermute(lax.slice_in_dim(block, 0, width, axis=dim), axis, backward)
        block = jnp.concatenate([low, block, high], axis=dim)
    return block


def coarse_update(padded):
    surf = padded[0]
    total = padded[1]
    rows_flux = padded[2]
    cols_flux = padded[3]
    face_rows = jnp.minimum(total[:-1, 1:-1], total[1:, 1:-1])
    new_rows = jnp.minimum(face_rows, 1.0) * (
        rows_flux[:-1, 1:-1]
        - coarse_tick * gravity * face_rows * (surf[1:, 1:-1] - surf[:-1, 1:-1]) / coarse_spacing
    )
    face_cols = jnp.minimum(total[1:-1, :-1], total[1:-1, 1:])
    new_cols = jnp.minimum(face_cols, 1.0) * (
        cols_flux[1:-1, :-1]
        - coarse_tick * gravity * face_cols * (surf[1:-1, 1:] - surf[1:-1, :-1]) / coarse_spacing
    )
    surface = surf[1:-1, 1:-1] - coarse_tick / coarse_spacing * (
        new_rows[1:] - new_rows[:-1] + (new_cols[:, 1:] - new_cols[:, :-1])
    )
    return (surface, new_rows[1:], new_cols[:, 1:])


def face_flux(flux_old, face_depth, slope, rough, fine_tick):
    wetness = jnp.minimum(face_depth / dry_depth, 1.0)
    driven = flux_old - fine_tick * gravity * face_depth * slope / fine_spacing
    friction = 1.0 + fine_tick * gravity * rough * rough * jnp.abs(flux_old) / jnp.power(
        jnp.maximum(face_depth, depth_floor), 7.0 / 3.0
    )
    return wetness * driven / friction


def fine_faces(water_pad, bed_pad, rough_pad, rows_pad, cols_pad, fine_tick):
    surf = bed_pad + water_pad
    depth_rows = jnp.maximum(
        jnp.maximum(surf[:-1, 1:-1], surf[1:, 1:-1])
        - jnp.maximum(bed_pad[:-1, 1:-1], bed_pad[1:, 1:-1]),
        0.0,
    )
    rough_rows = 0.5 * (rough_pad[:-1, 1:-1] + rough_pad[1:, 1:-1])
    new_rows = face_flux(
        rows_pad[:-1, 1:-1], depth_rows, surf[1:, 1:-1] - surf[:-1, 1:-1], rough_rows, fine_tick
    )
    depth_cols = jnp.maximum(
        jnp.maximum(surf[1:-1, :-1], surf[1:-1, 1:])
        - jnp.maximum(bed_pad[1:-1, :-1], bed_pad[1:-1, 1:]),
        0.0,
    )
    rough_cols = 0.5 * (rough_pad[1:-1, :-1] + rough_pad[1:-1, 1:])
    new_cols = face_flux(
        cols_pad[1:-1, :-1], depth_cols, surf[1:-1, 1:] - surf[1:-1, :-1], rough_cols, fine_tick
    )
    return (new_rows, new_cols)


def open_boundary(water_top, bed_top, bnd_surface, bnd_velocity):
    return water_top * bnd_velocity + jnp.sqrt(gravity * jnp.maximum(water_top, depth_floor)) * (
        bnd_surface - (bed_top + water_top)
    )


def blend(levels_stack, fine_index):
    lower = fine_index // SUB
    weight = (fine_index % SUB + 1) / SUB
    return (1.0 - weight) * levels_stack[lower] + weight * levels_stack[lower + 1]


def per_device(c_eta, c_flux, c_depth, f_bed, f_depth, f_wet, f_class, manning, nest_map):
    row_index = lax.axis_index("rows")
    col_index = lax.axis_index("cols")
    row_count = lax.axis_size("rows")
    col_count = lax.axis_size("cols")
    tile_rows, tile_cols = c_eta.shape
    fine_rows_dev, fine_cols_dev = f_bed.shape
    coarse_width = tile_cols * col_count
    coarse_row = nest_map // coarse_width
    coarse_col = nest_map % coarse_width
    local_row = coarse_row - row_index * tile_rows
    local_col = coarse_col - col_index * tile_cols
    owned = (local_row >= 0) & (local_row < tile_rows) & (local_col >= 0) & (local_col < tile_cols)
    flat_index = jnp.where(owned, local_row * tile_cols + local_col, 0)
    owned_weight = jnp.where(owned, 1.0, 0.0)

    def sample(surface, rows_flux):
        velocity = rows_flux / (c_depth + surface)
        return jnp.stack(
            [
                jnp.take(surface.reshape(-1), flat_index) * owned_weight,
                jnp.take(velocity.reshape(-1), flat_index) * owned_weight,
            ]
        )

    surface = c_eta
    rows_flux = c_flux[0]
    cols_flux = c_flux[1]
    sampled = [sample(surface, rows_flux)]
    for coarse_index in range(CSTEPS):
        stacked = jnp.stack([surface, c_depth + surface, rows_flux, cols_flux])
        padded = padded_2(stacked, (("rows", 1), ("cols", 2)), 1)
        surface, rows_flux, cols_flux = coarse_update(padded)
        sampled.append(sample(surface, rows_flux))
    levels_stack = jnp.stack(sampled)
    per_step = jnp.stack([blend(levels_stack, fine_index) for fine_index in range(FSTEPS)])
    summed = lax.psum(per_step, ("rows", "cols"))
    boundary = lax.dynamic_slice_in_dim(summed, col_index * fine_cols_dev, fine_cols_dev, 2)
    roughness = jnp.zeros_like(f_bed)
    for class_index in range(NCLASS):
        roughness = jnp.where(f_class == class_index, manning[class_index], roughness)
    water = f_wet.astype(f_bed.dtype) * f_depth
    fine_rows = jnp.zeros_like(water)
    fine_cols = jnp.zeros_like(water)
    fine_tick = coarse_tick / SUB
    row_start = row_index * fine_rows_dev
    col_start = col_index * fine_cols_dev
    total_rows = fine_rows_dev * row_count
    total_cols = fine_cols_dev * col_count
    col_faces = col_start + jnp.arange(fine_cols_dev + 1)
    col_keep = jnp.where((col_faces == 0) | (col_faces == total_cols), 0.0, 1.0)[None, :]
    static_pad = padded_2(jnp.stack([f_bed, roughness]), (("rows", 1), ("cols", 2)), 1)
    bed_pad = static_pad[0]
    rough_pad = static_pad[1]
    row_faces = row_start + jnp.arange(fine_rows_dev + 1)
    row_keep = jnp.where(row_faces == total_rows, 0.0, 1.0)[:, None]
    at_top = row_index == 0
    for fine_index in range(FSTEPS):
        state_pad = padded_2(
            jnp.stack([water, fine_rows, fine_cols]), (("rows", 1), ("cols", 2)), 1
        )
        water_pad = state_pad[0]
        new_rows, new_cols = fine_faces(
            water_pad, bed_pad, rough_pad, state_pad[1], state_pad[2], fine_tick
        )
        new_rows = new_rows * row_keep
        new_cols = new_cols * col_keep
        top_flux = open_boundary(
            water_pad[1, 1:-1], bed_pad[1, 1:-1], boundary[fine_index, 0], boundary[fine_index, 1]
        )
        first_face = jnp.where(at_top, top_flux, new_rows[0])
        new_rows = jnp.concatenate([first_face[None, :], new_rows[1:]], axis=0)
        water = water_pad[1:-1, 1:-1] - fine_tick / fine_spacing * (
            new_rows[1:] - new_rows[:-1] + (new_cols[:, 1:] - new_cols[:, :-1])
        )
        fine_rows = new_rows[1:]
        fine_cols = new_cols[:, 1:]
    return (surface, water, jnp.stack([fine_rows, fine_cols]))


def solution(mesh):
    in_specs = (
        P("rows", "cols"),
        P(None, "rows", "cols"),
        P("rows", "cols"),
        P("rows", "cols"),
        P("rows", "cols"),
        P("rows", "cols"),
        P("rows", "cols"),
        P(),
        P(),
    )
    out_specs = (P("rows", "cols"), P("rows", "cols"), P(None, "rows", "cols"))
    return jax.shard_map(
        per_device, mesh=mesh, in_specs=in_specs, out_specs=out_specs, check_vma=False
    )
```

profile of v0, /device:TPU:1, one launch (start us, length us, event | category | flops | bytes accessed | tf_op | source)
XLA Modules:
  0.0 376.3 jit_solution(18096316524865931316)
XLA Ops:
  8.4 3.9 %collective-permute-start = (f32[4,1,256]{2,1,0:T(1,128)S(1)}, f32[4,1,256]{2,1,0:T(1,128)S(1)}, u32[]{:S(2)}, u32[]{:S(2)}) collective-permute-start(f32[4,1,256]{2,1,0:T(1,128)S(1)} %get-tuple-element.32), channel_id=1, source_target_pairs={{0,8},{8,16},{16,24},{1,9},{9,17},{17,25},{2,10},{10,18},{18,26},{... | collective-permute-start | bytes 12296 | tf_op jit(solution)/shard_map/ppermute | solution.py:23
  14.4 7.0 %select_bitcast_fusion = f32[1,32,256]{2,1,0:T(8,128)S(1)} fusion(s32[32,256]{1,0:T(8,128)S(1)} %copy-done.9, f32[]{:T(128)} %bitcast.27, f32[]{:T(128)} %bitcast.26, f32[]{:T(128)} %bitcast.25, f32[]{:T(128)} %bitcast.24, f32[]{:T(128)} %bitcast.23, f32[]{:T(128)} %bitcast.22, f32[]{:T(128)} %bitcast.21, f32[]{:T(128)} %bitcast.20, f32[]{:T(128)} %bitcast.19, ...), kind=kLoop, calls=%fused_computation.156 | loop fusion | flops 180224 | bytes 65580 | tf_op jit(solution)/shard_map/stack | solution.py:147
  21.4 4.0 %collective-permute-start.12 = (f32[2,1,256]{2,1,0:T(1,128)S(1)}, f32[2,1,256]{2,1,0:T(1,128)S(1)}, u32[]{:S(2)}, u32[]{:S(2)}) collective-permute-start(f32[2,1,256]{2,1,0:T(1,128)S(1)} %get-tuple-element.82), channel_id=1, source_target_pairs={{0,8},{8,16},{16,24},{1,9},{9,17},{17,25},{2,10},{10,18},{18,26},{... | collective-permute-start | bytes 6152 | tf_op jit(solution)/shard_map/ppermute | solution.py:23
  26.8 4.7 %collective-permute-start.8 = (f32[3,1,256]{2,1,0:T(1,128)S(1)}, f32[3,1,256]{2,1,0:T(1,128)S(1)}, u32[]{:S(2)}, u32[]{:S(2)}) collective-permute-start(f32[3,1,256]{2,1,0:T(1,128)S(1)} %get-tuple-element.108), channel_id=1, source_target_pairs={{0,8},{8,16},{16,24},{1,9},{9,17},{17,25},{2,10},{10,18},{18,26},{... | collective-permute-start | bytes 9224 | tf_op jit(solution)/shard_map/ppermute | solution.py:23
  32.3 11.8 %gather_fusion.1 = f32[2048]{0:T(1024)S(1)} fusion(f32[32768]{0:T(1024)S(1)} %bitcast.271, s32[2048]{0:T(1024)S(1)} %get-tuple-element.10), kind=kCustom, calls=%fused_computation.1.clone | custom fusion | bytes 24576 | tf_op jit(solution)/shard_map/jit(_take)/gather | solution.py:117
  44.1 11.8 %gather_fusion = f32[2048]{0:T(1024)S(1)} fusion(f32[32768]{0:T(1024)S(1)} %bitcast.272, s32[2048]{0:T(1024)S(1)} %get-tuple-element.10), kind=kCustom, calls=%fused_computation.clone | custom fusion | bytes 24576 | tf_op jit(solution)/shard_map/jit(_take)/gather | solution.py:116
  56.0 4.9 %collective-permute-start.14 = (f32[2,34,1]{2,1,0:T(8,128)S(1)}, f32[2,34,1]{2,1,0:T(8,128)S(1)}, u32[]{:S(2)}, u32[]{:S(2)}) collective-permute-start(f32[2,34,1]{2,1,0:T(8,128)S(1)} %get-tuple-element.80), channel_id=1, source_target_pairs={{0,1},{1,2},{2,3},{3,4},{4,5},{5,6},{6,7},{8,9},{9,10},{10,11},{11... | collective-permute-start | bytes 824 | tf_op jit(solution)/shard_map/ppermute | solution.py:23
  60.9 1.9 collective-permute-start.15
  64.2 2.3 collective-permute-done.15
  68.5 4.5 %collective-permute-start.10 = (f32[3,34,1]{2,1,0:T(8,128)S(1)}, f32[3,34,1]{2,1,0:T(8,128)S(1)}, u32[]{:S(2)}, u32[]{:S(2)}) collective-permute-start(f32[3,34,1]{2,1,0:T(8,128)S(1)} %get-tuple-element.68), channel_id=1, source_target_pairs={{0,1},{1,2},{2,3},{3,4},{4,5},{5,6},{6,7},{8,9},{9,10},{10,11},{11... | collective-permute-start | bytes 1232 | tf_op jit(solution)/shard_map/ppermute | solution.py:23
  73.0 1.9 collective-permute-start.11
  75.0 3.6 collective-permute-done.11
  78.9 1.9 collective-permute-start.2
  80.9 2.4 collective-permute-start.3
  84.3 4.4 %collective-permute-done.3 = f32[4,130,1]{2,1,0:T(8,128)S(1)} collective-permute-done((f32[4,130,1]{2,1,0:T(8,128)S(1)}, f32[4,130,1]{2,1,0:T(8,128)S(1)}, u32[]{:S(2)}, u32[]{:S(2)}) %collective-permute-start.3) | collective-permute-done | bytes 2112 | tf_op jit(solution)/shard_map/ppermute | solution.py:26
  90.5 4.5 %collective-permute-start.4 = (f32[4,1,256]{2,1,0:T(1,128)S(1)}, f32[4,1,256]{2,1,0:T(1,128)S(1)}, u32[]{:S(2)}, u32[]{:S(2)}) collective-permute-start(f32[4,1,256]{2,1,0:T(1,128)S(1)} %get-tuple-element.30), channel_id=1, source_target_pairs={{0,8},{8,16},{16,24},{1,9},{9,17},{17,25},{2,10},{10,18},{18,26},{... | collective-permute-start | bytes 12296 | tf_op jit(solution)/shard_map/ppermute | solution.py:23
  96.5 2.9 collective-permute-done.5
  99.6 3.2 collective-permute-start.6
  102.8 1.9 collective-permute-start.7
  105.0 11.8 %gather_fusion.2 = f32[2048]{0:T(1024)S(1)} fusion(f32[32768]{0:T(1024)S(1)} %bitcast.275, s32[2048]{0:T(1024)S(1)} %get-tuple-element.10), kind=kCustom, calls=%fused_computation.2.clone | custom fusion | bytes 24576 | tf_op jit(solution)/shard_map/jit(_take)/gather | solution.py:116
  116.8 11.8 %gather_fusion.3 = f32[2048]{0:T(1024)S(1)} fusion(f32[32768]{0:T(1024)S(1)} %bitcast.274, s32[2048]{0:T(1024)S(1)} %get-tuple-element.10), kind=kCustom, calls=%fused_computation.3.clone | custom fusion | bytes 24576 | tf_op jit(solution)/shard_map/jit(_take)/gather | solution.py:117
  130.4 11.8 %gather_fusion.4 = f32[2048]{0:T(1024)S(1)} fusion(f32[32768]{0:T(1024)S(1)} %bitcast.276, s32[2048]{0:T(1024)S(1)} %get-tuple-element.10), kind=kCustom, calls=%fused_computation.4.clone | custom fusion | bytes 24576 | tf_op jit(solution)/shard_map/jit(_take)/gather | solution.py:116
  142.2 11.8 %gather_fusion.5 = f32[2048]{0:T(1024)S(1)} fusion(f32[32768]{0:T(1024)S(1)} %bitcast.273, s32[2048]{0:T(1024)S(1)} %get-tuple-element.10), kind=kCustom, calls=%fused_computation.5.clone | custom fusion | bytes 24576 | tf_op jit(solution)/shard_map/jit(_take)/gather | solution.py:117
  155.0 120.0 %all-reduce.3.cloned.1.call-done = f32[6,2,2048]{2,1,0:T(2,128)} async-done(((f32[6,2,2048]{2,1,0:T(2,128)}), f32[6,2,2048]{2,1,0:T(2,128)}) %all-reduce.3.cloned.1.call-update) | async-done | bytes 98320 | tf_op jit(solution)/shard_map/psum | solution.py:132
  276.0 3.1 collective-permute-start.16
  280.4 3.0 collective-permute-done.17
  283.5 7.1 %collective-permute-start.18 = (f32[3,34,1]{2,1,0:T(8,128)S(1)}, f32[3,34,1]{2,1,0:T(8,128)S(1)}, u32[]{:S(2)}, u32[]{:S(2)}) collective-permute-start(f32[3,34,1]{2,1,0:T(8,128)S(1)} %get-tuple-element.64), channel_id=1, source_target_pairs={{0,1},{1,2},{2,3},{3,4},{4,5},{5,6},{6,7},{8,9},{9,10},{10,11},{11... | collective-permute-start | bytes 1232 | tf_op jit(solution)/shard_map/ppermute | solution.py:23
  290.7 1.9 collective-permute-start.19
  292.6 3.6 collective-permute-done.19
  297.7 4.0 %collective-permute-start.20 = (f32[3,1,256]{2,1,0:T(1,128)S(1)}, f32[3,1,256]{2,1,0:T(1,128)S(1)}, u32[]{:S(2)}, u32[]{:S(2)}) collective-permute-start(f32[3,1,256]{2,1,0:T(1,128)S(1)} %get-tuple-element.76), channel_id=1, source_target_pairs={{0,8},{8,16},{16,24},{1,9},{9,17},{17,25},{2,10},{10,18},{18,26},{... | collective-permute-start | bytes 9224 | tf_op jit(solution)/shard_map/ppermute | solution.py:23
  303.0 3.0 collective-permute-done.21
  306.1 3.3 collective-permute-start.22
  309.4 1.9 collective-permute-start.23
  311.4 3.6 collective-permute-done.23
  316.4 2.5 collective-permute-start.24
  320.3 3.0 collective-permute-done.25
  323.4 3.3 collective-permute-start.26
  326.7 1.9 collective-permute-start.27
  328.6 3.6 collective-permute-done.27
  333.7 2.5 collective-permute-start.28
  337.6 3.0 collective-permute-done.29
  340.7 3.3 collective-permute-start.30
  344.0 1.9 collective-permute-start.31
  345.9 3.6 collective-permute-done.31
  351.0 2.5 collective-permute-start.32
  354.8 3.0 collective-permute-done.33
  357.9 3.3 collective-permute-start.34
  363.2 3.6 collective-permute-done.35
  (166 shorter events, 34.6 us)
Async XLA Ops:
  7.2 1.2 copy-start
  7.2 1.2 copy-start.1
  7.2 267.9 %all-reduce.3.cloned.1.call-start = ((), (), s32[]{:S(2)}) async-start(), calls=%async_computation | async-start | bytes 196608 | tf_op jit(solution)/shard_map/psum | solution.py:132
  8.4 5.3 %copy-start.6 = (f32[11]{0:T(128)S(1)}, f32[11]{0:T(128)}, u32[]{:S(2)}) copy-start(f32[11]{0:T(128)} %param.18) | copy-start | bytes 136
  8.4 6.0 %copy-start.9 = (s32[32,256]{1,0:T(8,128)S(1)}, s32[32,256]{1,0:T(8,128)}, u32[]{:S(2)}) copy-start(s32[32,256]{1,0:T(8,128)} %param.17) | copy-start | bytes 98308
  8.4 70.3 %collective-permute-start = (f32[4,1,256]{2,1,0:T(1,128)S(1)}, f32[4,1,256]{2,1,0:T(1,128)S(1)}, u32[]{:S(2)}, u32[]{:S(2)}) collective-permute-start(f32[4,1,256]{2,1,0:T(1,128)S(1)} %get-tuple-element.32), channel_id=1, source_target_pairs={{0,8},{8,16},{16,24},{1,9},{9,17},{17,25},{2,10},{10,18},{18,26},{... | collective-permute-start | bytes 12296 | tf_op jit(solution)/shard_map/ppermute | solution.py:23
  12.4 66.4 %collective-permute-start.1 = (f32[4,1,256]{2,1,0:T(1,128)S(1)}, f32[4,1,256]{2,1,0:T(1,128)S(1)}, u32[]{:S(2)}, u32[]{:S(2)}) collective-permute-start(f32[4,1,256]{2,1,0:T(1,128)S(1)} %get-tuple-element.33), channel_id=1, source_target_pairs={{8,0},{16,8},{24,16},{9,1},{17,9},{25,17},{10,2},{18,10},{26,18},{... | collective-permute-start | bytes 12296 | tf_op jit(solution)/shard_map/ppermute | solution.py:26
  14.4 7.0 %copy-start.4 = (f32[32,256]{1,0:T(8,128)S(1)}, f32[32,256]{1,0:T(8,128)}, u32[]{:S(2)}) copy-start(f32[32,256]{1,0:T(8,128)} %param.14) | copy-start | bytes 98308
  21.4 5.3 %copy-start.7 = (f32[32,256]{1,0:T(8,128)S(1)}, f32[32,256]{1,0:T(8,128)}, u32[]{:S(2)}) copy-start(f32[32,256]{1,0:T(8,128)} %param.15) | copy-start | bytes 98308
  21.4 5.3 %copy-start.8 = (s32[32,256]{1,0:T(8,128)S(1)}, s32[32,256]{1,0:T(8,128)}, u32[]{:S(2)}) copy-start(s32[32,256]{1,0:T(8,128)} %param.16) | copy-start | bytes 98308
  21.4 34.5 %collective-permute-start.12 = (f32[2,1,256]{2,1,0:T(1,128)S(1)}, f32[2,1,256]{2,1,0:T(1,128)S(1)}, u32[]{:S(2)}, u32[]{:S(2)}) collective-permute-start(f32[2,1,256]{2,1,0:T(1,128)S(1)} %get-tuple-element.82), channel_id=1, source_target_pairs={{0,8},{8,16},{16,24},{1,9},{9,17},{17,25},{2,10},{10,18},{18,26},{... | collective-permute-start | bytes 6152 | tf_op jit(solution)/shard_map/ppermute | solution.py:23
  25.4 30.5 %collective-permute-start.13 = (f32[2,1,256]{2,1,0:T(1,128)S(1)}, f32[2,1,256]{2,1,0:T(1,128)S(1)}, u32[]{:S(2)}, u32[]{:S(2)}) collective-permute-start(f32[2,1,256]{2,1,0:T(1,128)S(1)} %get-tuple-element.83), channel_id=1, source_target_pairs={{8,0},{16,8},{24,16},{9,1},{17,9},{25,17},{10,2},{18,10},{26,18},{... | collective-permute-start | bytes 6152 | tf_op jit(solution)/shard_map/ppermute | solution.py:26
  26.8 39.8 %collective-permute-start.8 = (f32[3,1,256]{2,1,0:T(1,128)S(1)}, f32[3,1,256]{2,1,0:T(1,128)S(1)}, u32[]{:S(2)}, u32[]{:S(2)}) collective-permute-start(f32[3,1,256]{2,1,0:T(1,128)S(1)} %get-tuple-element.108), channel_id=1, source_target_pairs={{0,8},{8,16},{16,24},{1,9},{9,17},{17,25},{2,10},{10,18},{18,26},{... | collective-permute-start | bytes 9224 | tf_op jit(solution)/shard_map/ppermute | solution.py:23
  31.4 0.7 copy-start.10
  56.0 6.8 %collective-permute-start.14 = (f32[2,34,1]{2,1,0:T(8,128)S(1)}, f32[2,34,1]{2,1,0:T(8,128)S(1)}, u32[]{:S(2)}, u32[]{:S(2)}) collective-permute-start(f32[2,34,1]{2,1,0:T(8,128)S(1)} %get-tuple-element.80), channel_id=1, source_target_pairs={{0,1},{1,2},{2,3},{3,4},{4,5},{5,6},{6,7},{8,9},{9,10},{10,11},{11... | collective-permute-start | bytes 824 | tf_op jit(solution)/shard_map/ppermute | solution.py:23
  60.9 5.5 %collective-permute-start.15 = (f32[2,34,1]{2,1,0:T(8,128)S(1)}, f32[2,34,1]{2,1,0:T(8,128)S(1)}, u32[]{:S(2)}, u32[]{:S(2)}) collective-permute-start(f32[2,34,1]{2,1,0:T(8,128)S(1)} %get-tuple-element.81), channel_id=1, source_target_pairs={{1,0},{2,1},{3,2},{4,3},{5,4},{6,5},{7,6},{9,8},{10,9},{11,10},{12... | collective-permute-start | bytes 824 | tf_op jit(solution)/shard_map/ppermute | solution.py:26
  62.9 5.5 %collective-permute-start.9 = (f32[3,1,256]{2,1,0:T(1,128)S(1)}, f32[3,1,256]{2,1,0:T(1,128)S(1)}, u32[]{:S(2)}, u32[]{:S(2)}) collective-permute-start(f32[3,1,256]{2,1,0:T(1,128)S(1)} %get-tuple-element.109), channel_id=1, source_target_pairs={{8,0},{16,8},{24,16},{9,1},{17,9},{25,17},{10,2},{18,10},{26,18},{... | collective-permute-start | bytes 9224 | tf_op jit(solution)/shard_map/ppermute | solution.py:26
  68.5 6.5 %collective-permute-start.10 = (f32[3,34,1]{2,1,0:T(8,128)S(1)}, f32[3,34,1]{2,1,0:T(8,128)S(1)}, u32[]{:S(2)}, u32[]{:S(2)}) collective-permute-start(f32[3,34,1]{2,1,0:T(8,128)S(1)} %get-tuple-element.68), channel_id=1, source_target_pairs={{0,1},{1,2},{2,3},{3,4},{4,5},{5,6},{6,7},{8,9},{9,10},{10,11},{11... | collective-permute-start | bytes 1232 | tf_op jit(solution)/shard_map/ppermute | solution.py:23
  73.0 5.5 %collective-permute-start.11 = (f32[3,34,1]{2,1,0:T(8,128)S(1)}, f32[3,34,1]{2,1,0:T(8,128)S(1)}, u32[]{:S(2)}, u32[]{:S(2)}) collective-permute-start(f32[3,34,1]{2,1,0:T(8,128)S(1)} %get-tuple-element.69), channel_id=1, source_target_pairs={{1,0},{2,1},{3,2},{4,3},{5,4},{6,5},{7,6},{9,8},{10,9},{11,10},{12... | collective-permute-start | bytes 1232 | tf_op jit(solution)/shard_map/ppermute | solution.py:26
  78.9 5.4 %collective-permute-start.2 = (f32[4,130,1]{2,1,0:T(8,128)S(1)}, f32[4,130,1]{2,1,0:T(8,128)S(1)}, u32[]{:S(2)}, u32[]{:S(2)}) collective-permute-start(f32[4,130,1]{2,1,0:T(8,128)S(1)} %get-tuple-element.28), channel_id=1, source_target_pairs={{0,1},{1,2},{2,3},{3,4},{4,5},{5,6},{6,7},{8,9},{9,10},{10,11},{11... | collective-permute-start | bytes 6248 | tf_op jit(solution)/shard_map/ppermute | solution.py:23
  80.9 7.9 %collective-permute-start.3 = (f32[4,130,1]{2,1,0:T(8,128)S(1)}, f32[4,130,1]{2,1,0:T(8,128)S(1)}, u32[]{:S(2)}, u32[]{:S(2)}) collective-permute-start(f32[4,130,1]{2,1,0:T(8,128)S(1)} %get-tuple-element.29), channel_id=1, source_target_pairs={{1,0},{2,1},{3,2},{4,3},{5,4},{6,5},{7,6},{9,8},{10,9},{11,10},{12... | collective-permute-start | bytes 6248 | tf_op jit(solution)/shard_map/ppermute | solution.py:26
  89.4 0.9 copy-start.2
  90.5 6.0 %collective-permute-start.4 = (f32[4,1,256]{2,1,0:T(1,128)S(1)}, f32[4,1,256]{2,1,0:T(1,128)S(1)}, u32[]{:S(2)}, u32[]{:S(2)}) collective-permute-start(f32[4,1,256]{2,1,0:T(1,128)S(1)} %get-tuple-element.30), channel_id=1, source_target_pairs={{0,8},{8,16},{16,24},{1,9},{9,17},{17,25},{2,10},{10,18},{18,26},{... | collective-permute-start | bytes 12296 | tf_op jit(solution)/shard_map/ppermute | solution.py:23
  95.1 4.4 %collective-permute-start.5 = (f32[4,1,256]{2,1,0:T(1,128)S(1)}, f32[4,1,256]{2,1,0:T(1,128)S(1)}, u32[]{:S(2)}, u32[]{:S(2)}) collective-permute-start(f32[4,1,256]{2,1,0:T(1,128)S(1)} %get-tuple-element.31), channel_id=1, source_target_pairs={{8,0},{16,8},{24,16},{9,1},{17,9},{25,17},{10,2},{18,10},{26,18},{... | collective-permute-start | bytes 12296 | tf_op jit(solution)/shard_map/ppermute | solution.py:26
  99.6 29.0 %collective-permute-start.6 = (f32[4,130,1]{2,1,0:T(8,128)S(1)}, f32[4,130,1]{2,1,0:T(8,128)S(1)}, u32[]{:S(2)}, u32[]{:S(2)}) collective-permute-start(f32[4,130,1]{2,1,0:T(8,128)S(1)} %get-tuple-element.26), channel_id=1, source_target_pairs={{0,1},{1,2},{2,3},{3,4},{4,5},{5,6},{6,7},{8,9},{9,10},{10,11},{11... | collective-permute-start | bytes 6248 | tf_op jit(solution)/shard_map/ppermute | solution.py:23
  102.8 25.8 %collective-permute-start.7 = (f32[4,130,1]{2,1,0:T(8,128)S(1)}, f32[4,130,1]{2,1,0:T(8,128)S(1)}, u32[]{:S(2)}, u32[]{:S(2)}) collective-permute-start(f32[4,130,1]{2,1,0:T(8,128)S(1)} %get-tuple-element.27), channel_id=1, source_target_pairs={{1,0},{2,1},{3,2},{4,3},{5,4},{6,5},{7,6},{9,8},{10,9},{11,10},{12... | collective-permute-start | bytes 6248 | tf_op jit(solution)/shard_map/ppermute | solution.py:26
  129.7 0.7 copy-start.3
  154.4 0.6 copy-start.5
  276.0 4.4 %collective-permute-start.16 = (f32[3,1,256]{2,1,0:T(1,128)S(1)}, f32[3,1,256]{2,1,0:T(1,128)S(1)}, u32[]{:S(2)}, u32[]{:S(2)}) collective-permute-start(f32[3,1,256]{2,1,0:T(1,128)S(1)} %get-tuple-element.78), channel_id=1, source_target_pairs={{0,8},{8,16},{16,24},{1,9},{9,17},{17,25},{2,10},{10,18},{18,26},{... | collective-permute-start | bytes 9224 | tf_op jit(solution)/shard_map/ppermute | solution.py:23
  279.1 4.3 %collective-permute-start.17 = (f32[3,1,256]{2,1,0:T(1,128)S(1)}, f32[3,1,256]{2,1,0:T(1,128)S(1)}, u32[]{:S(2)}, u32[]{:S(2)}) collective-permute-start(f32[3,1,256]{2,1,0:T(1,128)S(1)} %get-tuple-element.79), channel_id=1, source_target_pairs={{8,0},{16,8},{24,16},{9,1},{17,9},{25,17},{10,2},{18,10},{26,18},{... | collective-permute-start | bytes 9224 | tf_op jit(solution)/shard_map/ppermute | solution.py:26
  283.5 9.1 %collective-permute-start.18 = (f32[3,34,1]{2,1,0:T(8,128)S(1)}, f32[3,34,1]{2,1,0:T(8,128)S(1)}, u32[]{:S(2)}, u32[]{:S(2)}) collective-permute-start(f32[3,34,1]{2,1,0:T(8,128)S(1)} %get-tuple-element.64), channel_id=1, source_target_pairs={{0,1},{1,2},{2,3},{3,4},{4,5},{5,6},{6,7},{8,9},{9,10},{10,11},{11... | collective-permute-start | bytes 1232 | tf_op jit(solution)/shard_map/ppermute | solution.py:23
  290.7 5.5 %collective-permute-start.19 = (f32[3,34,1]{2,1,0:T(8,128)S(1)}, f32[3,34,1]{2,1,0:T(8,128)S(1)}, u32[]{:S(2)}, u32[]{:S(2)}) collective-permute-start(f32[3,34,1]{2,1,0:T(8,128)S(1)} %get-tuple-element.65), channel_id=1, source_target_pairs={{1,0},{2,1},{3,2},{4,3},{5,4},{6,5},{7,6},{9,8},{10,9},{11,10},{12... | collective-permute-start | bytes 1232 | tf_op jit(solution)/shard_map/ppermute | solution.py:26
  297.7 5.3 %collective-permute-start.20 = (f32[3,1,256]{2,1,0:T(1,128)S(1)}, f32[3,1,256]{2,1,0:T(1,128)S(1)}, u32[]{:S(2)}, u32[]{:S(2)}) collective-permute-start(f32[3,1,256]{2,1,0:T(1,128)S(1)} %get-tuple-element.76), channel_id=1, source_target_pairs={{0,8},{8,16},{16,24},{1,9},{9,17},{17,25},{2,10},{10,18},{18,26},{... | collective-permute-start | bytes 9224 | tf_op jit(solution)/shard_map/ppermute | solution.py:23
  301.7 4.3 %collective-permute-start.21 = (f32[3,1,256]{2,1,0:T(1,128)S(1)}, f32[3,1,256]{2,1,0:T(1,128)S(1)}, u32[]{:S(2)}, u32[]{:S(2)}) collective-permute-start(f32[3,1,256]{2,1,0:T(1,128)S(1)} %get-tuple-element.77), channel_id=1, source_target_pairs={{8,0},{16,8},{24,16},{9,1},{17,9},{25,17},{10,2},{18,10},{26,18},{... | collective-permute-start | bytes 9224 | tf_op jit(solution)/shard_map/ppermute | solution.py:26
  306.1 5.2 %collective-permute-start.22 = (f32[3,34,1]{2,1,0:T(8,128)S(1)}, f32[3,34,1]{2,1,0:T(8,128)S(1)}, u32[]{:S(2)}, u32[]{:S(2)}) collective-permute-start(f32[3,34,1]{2,1,0:T(8,128)S(1)} %get-tuple-element.62), channel_id=1, source_target_pairs={{0,1},{1,2},{2,3},{3,4},{4,5},{5,6},{6,7},{8,9},{9,10},{10,11},{11... | collective-permute-start | bytes 1232 | tf_op jit(solution)/shard_map/ppermute | solution.py:23
  309.4 5.5 %collective-permute-start.23 = (f32[3,34,1]{2,1,0:T(8,128)S(1)}, f32[3,34,1]{2,1,0:T(8,128)S(1)}, u32[]{:S(2)}, u32[]{:S(2)}) collective-permute-start(f32[3,34,1]{2,1,0:T(8,128)S(1)} %get-tuple-element.63), channel_id=1, source_target_pairs={{1,0},{2,1},{3,2},{4,3},{5,4},{6,5},{7,6},{9,8},{10,9},{11,10},{12... | collective-permute-start | bytes 1232 | tf_op jit(solution)/shard_map/ppermute | solution.py:26
  316.4 3.9 %collective-permute-start.24 = (f32[3,1,256]{2,1,0:T(1,128)S(1)}, f32[3,1,256]{2,1,0:T(1,128)S(1)}, u32[]{:S(2)}, u32[]{:S(2)}) collective-permute-start(f32[3,1,256]{2,1,0:T(1,128)S(1)} %get-tuple-element.74), channel_id=1, source_target_pairs={{0,8},{8,16},{16,24},{1,9},{9,17},{17,25},{2,10},{10,18},{18,26},{... | collective-permute-start | bytes 9224 | tf_op jit(solution)/shard_map/ppermute | solution.py:23
  319.0 4.3 %collective-permute-start.25 = (f32[3,1,256]{2,1,0:T(1,128)S(1)}, f32[3,1,256]{2,1,0:T(1,128)S(1)}, u32[]{:S(2)}, u32[]{:S(2)}) collective-permute-start(f32[3,1,256]{2,1,0:T(1,128)S(1)} %get-tuple-element.75), channel_id=1, source_target_pairs={{8,0},{16,8},{24,16},{9,1},{17,9},{25,17},{10,2},{18,10},{26,18},{... | collective-permute-start | bytes 9224 | tf_op jit(solution)/shard_map/ppermute | solution.py:26
  323.4 5.2 %collective-permute-start.26 = (f32[3,34,1]{2,1,0:T(8,128)S(1)}, f32[3,34,1]{2,1,0:T(8,128)S(1)}, u32[]{:S(2)}, u32[]{:S(2)}) collective-permute-start(f32[3,34,1]{2,1,0:T(8,128)S(1)} %get-tuple-element.60), channel_id=1, source_target_pairs={{0,1},{1,2},{2,3},{3,4},{4,5},{5,6},{6,7},{8,9},{9,10},{10,11},{11... | collective-permute-start | bytes 1232 | tf_op jit(solution)/shard_map/ppermute | solution.py:23
  326.7 5.5 %collective-permute-start.27 = (f32[3,34,1]{2,1,0:T(8,128)S(1)}, f32[3,34,1]{2,1,0:T(8,128)S(1)}, u32[]{:S(2)}, u32[]{:S(2)}) collective-permute-start(f32[3,34,1]{2,1,0:T(8,128)S(1)} %get-tuple-element.61), channel_id=1, source_target_pairs={{1,0},{2,1},{3,2},{4,3},{5,4},{6,5},{7,6},{9,8},{10,9},{11,10},{12... | collective-permute-start | bytes 1232 | tf_op jit(solution)/shard_map/ppermute | solution.py:26
  333.7 3.9 %collective-permute-start.28 = (f32[3,1,256]{2,1,0:T(1,128)S(1)}, f32[3,1,256]{2,1,0:T(1,128)S(1)}, u32[]{:S(2)}, u32[]{:S(2)}) collective-permute-start(f32[3,1,256]{2,1,0:T(1,128)S(1)} %get-tuple-element.72), channel_id=1, source_target_pairs={{0,8},{8,16},{16,24},{1,9},{9,17},{17,25},{2,10},{10,18},{18,26},{... | collective-permute-start | bytes 9224 | tf_op jit(solution)/shard_map/ppermute | solution.py:23
  336.2 4.3 %collective-permute-start.29 = (f32[3,1,256]{2,1,0:T(1,128)S(1)}, f32[3,1,256]{2,1,0:T(1,128)S(1)}, u32[]{:S(2)}, u32[]{:S(2)}) collective-permute-start(f32[3,1,256]{2,1,0:T(1,128)S(1)} %get-tuple-element.73), channel_id=1, source_target_pairs={{8,0},{16,8},{24,16},{9,1},{17,9},{25,17},{10,2},{18,10},{26,18},{... | collective-permute-start | bytes 9224 | tf_op jit(solution)/shard_map/ppermute | solution.py:26
  340.7 5.2 %collective-permute-start.30 = (f32[3,34,1]{2,1,0:T(8,128)S(1)}, f32[3,34,1]{2,1,0:T(8,128)S(1)}, u32[]{:S(2)}, u32[]{:S(2)}) collective-permute-start(f32[3,34,1]{2,1,0:T(8,128)S(1)} %get-tuple-element.58), channel_id=1, source_target_pairs={{0,1},{1,2},{2,3},{3,4},{4,5},{5,6},{6,7},{8,9},{9,10},{10,11},{11... | collective-permute-start | bytes 1232 | tf_op jit(solution)/shard_map/ppermute | solution.py:23
  344.0 5.5 %collective-permute-start.31 = (f32[3,34,1]{2,1,0:T(8,128)S(1)}, f32[3,34,1]{2,1,0:T(8,128)S(1)}, u32[]{:S(2)}, u32[]{:S(2)}) collective-permute-start(f32[3,34,1]{2,1,0:T(8,128)S(1)} %get-tuple-element.59), channel_id=1, source_target_pairs={{1,0},{2,1},{3,2},{4,3},{5,4},{6,5},{7,6},{9,8},{10,9},{11,10},{12... | collective-permute-start | bytes 1232 | tf_op jit(solution)/shard_map/ppermute | solution.py:26
  351.0 3.9 %collective-permute-start.32 = (f32[3,1,256]{2,1,0:T(1,128)S(1)}, f32[3,1,256]{2,1,0:T(1,128)S(1)}, u32[]{:S(2)}, u32[]{:S(2)}) collective-permute-start(f32[3,1,256]{2,1,0:T(1,128)S(1)} %get-tuple-element.70), channel_id=1, source_target_pairs={{0,8},{8,16},{16,24},{1,9},{9,17},{17,25},{2,10},{10,18},{18,26},{... | collective-permute-start | bytes 9224 | tf_op jit(solution)/shard_map/ppermute | solution.py:23
  353.5 4.3 %collective-permute-start.33 = (f32[3,1,256]{2,1,0:T(1,128)S(1)}, f32[3,1,256]{2,1,0:T(1,128)S(1)}, u32[]{:S(2)}, u32[]{:S(2)}) collective-permute-start(f32[3,1,256]{2,1,0:T(1,128)S(1)} %get-tuple-element.71), channel_id=1, source_target_pairs={{8,0},{16,8},{24,16},{9,1},{17,9},{25,17},{10,2},{18,10},{26,18},{... | collective-permute-start | bytes 9224 | tf_op jit(solution)/shard_map/ppermute | solution.py:26
  357.9 5.3 %collective-permute-start.34 = (f32[3,34,1]{2,1,0:T(8,128)S(1)}, f32[3,34,1]{2,1,0:T(8,128)S(1)}, u32[]{:S(2)}, u32[]{:S(2)}) collective-permute-start(f32[3,34,1]{2,1,0:T(8,128)S(1)} %get-tuple-element.56), channel_id=1, source_target_pairs={{0,1},{1,2},{2,3},{3,4},{4,5},{5,6},{6,7},{8,9},{9,10},{10,11},{11... | collective-permute-start | bytes 1232 | tf_op jit(solution)/shard_map/ppermute | solution.py:23
  361.3 5.5 %collective-permute-start.35 = (f32[3,34,1]{2,1,0:T(8,128)S(1)}, f32[3,34,1]{2,1,0:T(8,128)S(1)}, u32[]{:S(2)}, u32[]{:S(2)}) collective-permute-start(f32[3,34,1]{2,1,0:T(8,128)S(1)} %get-tuple-element.57), channel_id=1, source_target_pairs={{1,0},{2,1},{3,2},{4,3},{5,4},{6,5},{7,6},{9,8},{10,9},{11,10},{12... | collective-permute-start | bytes 1232 | tf_op jit(solution)/shard_map/ppermute | solution.py:26
Sparse Core Ops, SparseCore 0:
  155.1 119.8 all-reduce.2
where the time goes:
time: 378 us; the launch traced here: 376 us
  waiting for transfers between devices  169 us (45%)
  starting transfers between devices  96.1 us (25%)
  local copies, waits for them, and re-layouts  75.5 us (20%)
  other arithmetic  20.3 us (5%)
  between operations  15.2 us (4%)
    psum x1, waiting for transfers between devices, per_device(): summed = lax.psum(per_step, ('rows', 'cols'))  120 us
    ppermute x18, starting transfers between devices, padded_2(): lax.ppermute(lax.slice_in_dim(block, block.shape[dim] - width, None, axis...  66.7 us
    ppermute x18, waiting for transfers between devices, padded_2(): lax.ppermute(lax.slice_in_dim(block, 0, width, axis=dim), axis, backward)  48.1 us
    gather x3, local copies, waits for them, and re-layouts, sample(): jnp.take(velocity.reshape(-1), flat_index) * owned_weight  35.3 us
    gather x3, local copies, waits for them, and re-layouts, sample(): jnp.take(surface.reshape(-1), flat_index) * owned_weight  35.3 us
    ppermute x18, starting transfers between devices, padded_2(): lax.ppermute(lax.slice_in_dim(block, 0, width, axis=dim), axis, backward)  29.4 us
  transfers between devices with their start and end apart: 37, of which 17 were waited for; matrix products, arithmetic and copies ran while one was open for 15% of the time, Pallas kernels for 0%

commit v1 on v0

--- a/solution.py
+++ b/solution.py
@@ -2,6 +2,7 @@
 import jax.numpy as jnp
 from jax import lax
 from jax.sharding import PartitionSpec as P
+from jax.lax import psum
 
 NCLASS = 11
 CSTEPS = 2
@@ -13,6 +14,11 @@
 fine_spacing = 5.0
 depth_floor = 0.01
 dry_depth = 0.05
+
+
+def touch_column(in_array):
+    v_next = psum(in_array, "cols")
+    return psum(v_next, "rows")
 
 
 def padded_2(block, sides, width):
@@ -129,7 +135,7 @@
         sampled.append(sample(surface, rows_flux))
     levels_stack = jnp.stack(sampled)
     per_step = jnp.stack([blend(levels_stack, fine_index) for fine_index in range(FSTEPS)])
-    summed = lax.psum(per_step, ("rows", "cols"))
+    summed = touch_column(per_step)
     boundary = lax.dynamic_slice_in_dim(summed, col_index * fine_cols_dev, fine_cols_dev, 2)
     roughness = jnp.zeros_like(f_bed)
     for class_index in range(NCLASS):

time: 378 us -> 354 us (0.937)
  waiting for transfers between devices: 169 us -> 147 us
    psum x1 -> x2, waiting for transfers between devices: 120 us -> 97.3 us  [the longest x1 50.5 us: touch_column(): v_next = psum(in_array, 'cols')]
  transfers between devices with their start and end apart: 37 -> 38, of which waited for: 17 -> 18; matrix products, arithmetic and copies ran while one was open for 15% -> 16% of each run, Pallas kernels for 0% -> 0%
where the time goes in v1:
time: 354 us; the launch traced here: 352 us
  waiting for transfers between devices  147 us (42%)
  starting transfers between devices  94.4 us (27%)
  local copies, waits for them, and re-layouts  75.5 us (21%)
  other arithmetic  20.3 us (6%)
  between operations  15.2 us (4%)
    ppermute x18, starting transfers between devices, padded_2(): lax.ppermute(lax.slice_in_dim(block, block.shape[dim] - width, None, axis...  64.9 us
    psum x1, waiting for transfers between devices, touch_column(): v_next = psum(in_array, 'cols')  50.5 us
    ppermute x18, waiting for transfers between devices, padded_2(): lax.ppermute(lax.slice_in_dim(block, 0, width, axis=dim), axis, backward)  48.3 us
    psum x1, waiting for transfers between devices, touch_column(): return psum(v_next, 'rows')  46.8 us
    gather x3, local copies, waits for them, and re-layouts, sample(): jnp.take(velocity.reshape(-1), flat_index) * owned_weight  35.3 us
    gather x3, local copies, waits for them, and re-layouts, sample(): jnp.take(surface.reshape(-1), flat_index) * owned_weight  35.3 us
    ppermute x18, starting transfers between devices, padded_2(): lax.ppermute(lax.slice_in_dim(block, 0, width, axis=dim), axis, backward)  29.4 us
  transfers between devices with their start and end apart: 38, of which 18 were waited for; matrix products, arithmetic and copies ran while one was open for 16% of the time, Pallas kernels for 0%

profile of v1, /device:TPU:1, one launch (start us, length us, event | category | flops | bytes accessed | tf_op | source)
XLA Modules:
  0.0 352.1 jit_solution(9115187169508762083)
XLA Ops:
  8.4 3.9 %collective-permute-start = (f32[4,1,256]{2,1,0:T(1,128)S(1)}, f32[4,1,256]{2,1,0:T(1,128)S(1)}, u32[]{:S(2)}, u32[]{:S(2)}) collective-permute-start(f32[4,1,256]{2,1,0:T(1,128)S(1)} %get-tuple-element.32), channel_id=1, source_target_pairs={{0,8},{8,16},{16,24},{1,9},{9,17},{17,25},{2,10},{10,18},{18,26},{... | collective-permute-start | bytes 12296 | tf_op jit(solution)/shard_map/ppermute | solution.py:29
  14.4 7.0 %select_bitcast_fusion = f32[1,32,256]{2,1,0:T(8,128)S(1)} fusion(s32[32,256]{1,0:T(8,128)S(1)} %copy-done.9, f32[]{:T(128)} %bitcast.27, f32[]{:T(128)} %bitcast.26, f32[]{:T(128)} %bitcast.25, f32[]{:T(128)} %bitcast.24, f32[]{:T(128)} %bitcast.23, f32[]{:T(128)} %bitcast.22, f32[]{:T(128)} %bitcast.21, f32[]{:T(128)} %bitcast.20, f32[]{:T(128)} %bitcast.19, ...), kind=kLoop, calls=%fused_computation.156 | loop fusion | flops 180224 | bytes 65580 | tf_op jit(solution)/shard_map/stack | solution.py:153
  21.4 4.0 %collective-permute-start.12 = (f32[2,1,256]{2,1,0:T(1,128)S(1)}, f32[2,1,256]{2,1,0:T(1,128)S(1)}, u32[]{:S(2)}, u32[]{:S(2)}) collective-permute-start(f32[2,1,256]{2,1,0:T(1,128)S(1)} %get-tuple-element.82), channel_id=1, source_target_pairs={{0,8},{8,16},{16,24},{1,9},{9,17},{17,25},{2,10},{10,18},{18,26},{... | collective-permute-start | bytes 6152 | tf_op jit(solution)/shard_map/ppermute | solution.py:29
  26.8 4.7 %collective-permute-start.8 = (f32[3,1,256]{2,1,0:T(1,128)S(1)}, f32[3,1,256]{2,1,0:T(1,128)S(1)}, u32[]{:S(2)}, u32[]{:S(2)}) collective-permute-start(f32[3,1,256]{2,1,0:T(1,128)S(1)} %get-tuple-element.108), channel_id=1, source_target_pairs={{0,8},{8,16},{16,24},{1,9},{9,17},{17,25},{2,10},{10,18},{18,26},{... | collective-permute-start | bytes 9224 | tf_op jit(solution)/shard_map/ppermute | solution.py:29
  32.3 11.8 %gather_fusion.1 = f32[2048]{0:T(1024)S(1)} fusion(f32[32768]{0:T(1024)S(1)} %bitcast.271, s32[2048]{0:T(1024)S(1)} %get-tuple-element.10), kind=kCustom, calls=%fused_computation.1.clone | custom fusion | bytes 24576 | tf_op jit(solution)/shard_map/jit(_take)/gather | solution.py:123
  44.1 11.8 %gather_fusion = f32[2048]{0:T(1024)S(1)} fusion(f32[32768]{0:T(1024)S(1)} %bitcast.272, s32[2048]{0:T(1024)S(1)} %get-tuple-element.10), kind=kCustom, calls=%fused_computation.clone | custom fusion | bytes 24576 | tf_op jit(solution)/shard_map/jit(_take)/gather | solution.py:122
  56.0 4.9 %collective-permute-start.14 = (f32[2,34,1]{2,1,0:T(8,128)S(1)}, f32[2,34,1]{2,1,0:T(8,128)S(1)}, u32[]{:S(2)}, u32[]{:S(2)}) collective-permute-start(f32[2,34,1]{2,1,0:T(8,128)S(1)} %get-tuple-element.80), channel_id=1, source_target_pairs={{0,1},{1,2},{2,3},{3,4},{4,5},{5,6},{6,7},{8,9},{9,10},{10,11},{11... | collective-permute-start | bytes 824 | tf_op jit(solution)/shard_map/ppermute | solution.py:29
  60.9 1.9 collective-permute-start.15
  64.2 2.3 collective-permute-done.15
  68.5 4.5 %collective-permute-start.10 = (f32[3,34,1]{2,1,0:T(8,128)S(1)}, f32[3,34,1]{2,1,0:T(8,128)S(1)}, u32[]{:S(2)}, u32[]{:S(2)}) collective-permute-start(f32[3,34,1]{2,1,0:T(8,128)S(1)} %get-tuple-element.68), channel_id=1, source_target_pairs={{0,1},{1,2},{2,3},{3,4},{4,5},{5,6},{6,7},{8,9},{9,10},{10,11},{11... | collective-permute-start | bytes 1232 | tf_op jit(solution)/shard_map/ppermute | solution.py:29
  73.0 1.9 collective-permute-start.11
  75.0 3.6 %collective-permute-done.11 = f32[3,34,1]{2,1,0:T(8,128)S(1)} collective-permute-done((f32[3,34,1]{2,1,0:T(8,128)S(1)}, f32[3,34,1]{2,1,0:T(8,128)S(1)}, u32[]{:S(2)}, u32[]{:S(2)}) %collective-permute-start.11) | collective-permute-done | bytes 440 | tf_op jit(solution)/shard_map/ppermute | solution.py:32
  78.9 1.9 collective-permute-start.2
  80.8 2.4 collective-permute-start.3
  84.3 4.4 %collective-permute-done.3 = f32[4,130,1]{2,1,0:T(8,128)S(1)} collective-permute-done((f32[4,130,1]{2,1,0:T(8,128)S(1)}, f32[4,130,1]{2,1,0:T(8,128)S(1)}, u32[]{:S(2)}, u32[]{:S(2)}) %collective-permute-start.3) | collective-permute-done | bytes 2112 | tf_op jit(solution)/shard_map/ppermute | solution.py:32
  90.5 4.5 %collective-permute-start.4 = (f32[4,1,256]{2,1,0:T(1,128)S(1)}, f32[4,1,256]{2,1,0:T(1,128)S(1)}, u32[]{:S(2)}, u32[]{:S(2)}) collective-permute-start(f32[4,1,256]{2,1,0:T(1,128)S(1)} %get-tuple-element.30), channel_id=1, source_target_pairs={{0,8},{8,16},{16,24},{1,9},{9,17},{17,25},{2,10},{10,18},{18,26},{... | collective-permute-start | bytes 12296 | tf_op jit(solution)/shard_map/ppermute | solution.py:29
  96.4 3.0 collective-permute-done.5
  99.6 3.2 collective-permute-start.6
  102.8 1.9 collective-permute-start.7
  104.9 11.8 %gather_fusion.2 = f32[2048]{0:T(1024)S(1)} fusion(f32[32768]{0:T(1024)S(1)} %bitcast.275, s32[2048]{0:T(1024)S(1)} %get-tuple-element.10), kind=kCustom, calls=%fused_computation.2.clone | custom fusion | bytes 24576 | tf_op jit(solution)/shard_map/jit(_take)/gather | solution.py:122
  116.8 11.8 %gather_fusion.3 = f32[2048]{0:T(1024)S(1)} fusion(f32[32768]{0:T(1024)S(1)} %bitcast.274, s32[2048]{0:T(1024)S(1)} %get-tuple-element.10), kind=kCustom, calls=%fused_computation.3.clone | custom fusion | bytes 24576 | tf_op jit(solution)/shard_map/jit(_take)/gather | solution.py:123
  130.4 11.8 %gather_fusion.4 = f32[2048]{0:T(1024)S(1)} fusion(f32[32768]{0:T(1024)S(1)} %bitcast.276, s32[2048]{0:T(1024)S(1)} %get-tuple-element.10), kind=kCustom, calls=%fused_computation.4.clone | custom fusion | bytes 24576 | tf_op jit(solution)/shard_map/jit(_take)/gather | solution.py:122
  142.2 11.8 %gather_fusion.5 = f32[2048]{0:T(1024)S(1)} fusion(f32[32768]{0:T(1024)S(1)} %bitcast.273, s32[2048]{0:T(1024)S(1)} %get-tuple-element.10), kind=kCustom, calls=%fused_computation.5.clone | custom fusion | bytes 24576 | tf_op jit(solution)/shard_map/jit(_take)/gather | solution.py:123
  155.2 50.5 %all-reduce.4.cloned.1.call-done = f32[6,2,2048]{2,1,0:T(2,128)} async-done(((f32[6,2,2048]{2,1,0:T(2,128)}), f32[6,2,2048]{2,1,0:T(2,128)}) %all-reduce.4.cloned.1.call-update) | async-done | bytes 98320 | tf_op jit(solution)/shard_map/psum | solution.py:20
  205.8 46.8 %all-reduce.6.cloned.1.call-done = f32[6,2,2048]{2,1,0:T(2,128)} async-done(((f32[6,2,2048]{2,1,0:T(2,128)}), f32[6,2,2048]{2,1,0:T(2,128)}) %all-reduce.6.cloned.1.call-update) | async-done | bytes 98320 | tf_op jit(solution)/shard_map/psum | solution.py:21
  253.5 3.0 collective-permute-start.16
  257.8 3.0 collective-permute-done.17
  261.0 5.6 %collective-permute-start.18 = (f32[3,34,1]{2,1,0:T(8,128)S(1)}, f32[3,34,1]{2,1,0:T(8,128)S(1)}, u32[]{:S(2)}, u32[]{:S(2)}) collective-permute-start(f32[3,34,1]{2,1,0:T(8,128)S(1)} %get-tuple-element.64), channel_id=1, source_target_pairs={{0,1},{1,2},{2,3},{3,4},{4,5},{5,6},{6,7},{8,9},{9,10},{10,11},{11... | collective-permute-start | bytes 1232 | tf_op jit(solution)/shard_map/ppermute | solution.py:29
  266.5 1.9 collective-permute-start.19
  268.5 3.6 %collective-permute-done.19 = f32[3,34,1]{2,1,0:T(8,128)S(1)} collective-permute-done((f32[3,34,1]{2,1,0:T(8,128)S(1)}, f32[3,34,1]{2,1,0:T(8,128)S(1)}, u32[]{:S(2)}, u32[]{:S(2)}) %collective-permute-start.19) | collective-permute-done | bytes 440 | tf_op jit(solution)/shard_map/ppermute | solution.py:32
  273.5 3.9 %collective-permute-start.20 = (f32[3,1,256]{2,1,0:T(1,128)S(1)}, f32[3,1,256]{2,1,0:T(1,128)S(1)}, u32[]{:S(2)}, u32[]{:S(2)}) collective-permute-start(f32[3,1,256]{2,1,0:T(1,128)S(1)} %get-tuple-element.76), channel_id=1, source_target_pairs={{0,8},{8,16},{16,24},{1,9},{9,17},{17,25},{2,10},{10,18},{18,26},{... | collective-permute-start | bytes 9224 | tf_op jit(solution)/shard_map/ppermute | solution.py:29
  278.8 3.0 collective-permute-done.21
  281.9 3.3 collective-permute-start.22
  285.2 1.9 collective-permute-start.23
  287.1 3.6 %collective-permute-done.23 = f32[3,34,1]{2,1,0:T(8,128)S(1)} collective-permute-done((f32[3,34,1]{2,1,0:T(8,128)S(1)}, f32[3,34,1]{2,1,0:T(8,128)S(1)}, u32[]{:S(2)}, u32[]{:S(2)}) %collective-permute-start.23) | collective-permute-done | bytes 440 | tf_op jit(solution)/shard_map/ppermute | solution.py:32
  292.2 2.5 collective-permute-start.24
  296.0 3.0 collective-permute-done.25
  299.2 3.3 collective-permute-start.26
  302.5 1.9 collective-permute-start.27
  304.4 3.6 %collective-permute-done.27 = f32[3,34,1]{2,1,0:T(8,128)S(1)} collective-permute-done((f32[3,34,1]{2,1,0:T(8,128)S(1)}, f32[3,34,1]{2,1,0:T(8,128)S(1)}, u32[]{:S(2)}, u32[]{:S(2)}) %collective-permute-start.27) | collective-permute-done | bytes 440 | tf_op jit(solution)/shard_map/ppermute | solution.py:32
  309.5 2.5 collective-permute-start.28
  313.3 3.0 collective-permute-done.29
  316.4 3.3 collective-permute-start.30
  321.7 3.6 %collective-permute-done.31 = f32[3,34,1]{2,1,0:T(8,128)S(1)} collective-permute-done((f32[3,34,1]{2,1,0:T(8,128)S(1)}, f32[3,34,1]{2,1,0:T(8,128)S(1)}, u32[]{:S(2)}, u32[]{:S(2)}) %collective-permute-start.31) | collective-permute-done | bytes 440 | tf_op jit(solution)/shard_map/ppermute | solution.py:32
  326.7 2.5 collective-permute-start.32
  330.6 3.0 collective-permute-done.33
  333.7 3.3 collective-permute-start.34
  339.0 3.6 %collective-permute-done.35 = f32[3,34,1]{2,1,0:T(8,128)S(1)} collective-permute-done((f32[3,34,1]{2,1,0:T(8,128)S(1)}, f32[3,34,1]{2,1,0:T(8,128)S(1)}, u32[]{:S(2)}, u32[]{:S(2)}) %collective-permute-start.35) | collective-permute-done | bytes 440 | tf_op jit(solution)/shard_map/ppermute | solution.py:32
  (169 shorter events, 36.6 us)
Async XLA Ops:
  7.2 1.2 copy-start
  7.2 1.2 copy-start.1
  7.2 198.6 %all-reduce.4.cloned.1.call-start = ((), (), s32[]{:S(2)}) async-start(), calls=%async_computation | async-start | bytes 196608 | tf_op jit(solution)/shard_map/psum | solution.py:20
  8.4 5.3 %copy-start.6 = (f32[11]{0:T(128)S(1)}, f32[11]{0:T(128)}, u32[]{:S(2)}) copy-start(f32[11]{0:T(128)} %param.18) | copy-start | bytes 136
  8.4 6.0 %copy-start.9 = (s32[32,256]{1,0:T(8,128)S(1)}, s32[32,256]{1,0:T(8,128)}, u32[]{:S(2)}) copy-start(s32[32,256]{1,0:T(8,128)} %param.17) | copy-start | bytes 98308
  8.4 70.3 %collective-permute-start = (f32[4,1,256]{2,1,0:T(1,128)S(1)}, f32[4,1,256]{2,1,0:T(1,128)S(1)}, u32[]{:S(2)}, u32[]{:S(2)}) collective-permute-start(f32[4,1,256]{2,1,0:T(1,128)S(1)} %get-tuple-element.32), channel_id=1, source_target_pairs={{0,8},{8,16},{16,24},{1,9},{9,17},{17,25},{2,10},{10,18},{18,26},{... | collective-permute-start | bytes 12296 | tf_op jit(solution)/shard_map/ppermute | solution.py:29
  12.4 66.3 %collective-permute-start.1 = (f32[4,1,256]{2,1,0:T(1,128)S(1)}, f32[4,1,256]{2,1,0:T(1,128)S(1)}, u32[]{:S(2)}, u32[]{:S(2)}) collective-permute-start(f32[4,1,256]{2,1,0:T(1,128)S(1)} %get-tuple-element.33), channel_id=1, source_target_pairs={{8,0},{16,8},{24,16},{9,1},{17,9},{25,17},{10,2},{18,10},{26,18},{... | collective-permute-start | bytes 12296 | tf_op jit(solution)/shard_map/ppermute | solution.py:32
  14.4 7.0 %copy-start.4 = (f32[32,256]{1,0:T(8,128)S(1)}, f32[32,256]{1,0:T(8,128)}, u32[]{:S(2)}) copy-start(f32[32,256]{1,0:T(8,128)} %param.14) | copy-start | bytes 98308
  21.4 5.3 %copy-start.7 = (f32[32,256]{1,0:T(8,128)S(1)}, f32[32,256]{1,0:T(8,128)}, u32[]{:S(2)}) copy-start(f32[32,256]{1,0:T(8,128)} %param.15) | copy-start | bytes 98308
  21.4 5.3 %copy-start.8 = (s32[32,256]{1,0:T(8,128)S(1)}, s32[32,256]{1,0:T(8,128)}, u32[]{:S(2)}) copy-start(s32[32,256]{1,0:T(8,128)} %param.16) | copy-start | bytes 98308
  21.4 34.5 %collective-permute-start.12 = (f32[2,1,256]{2,1,0:T(1,128)S(1)}, f32[2,1,256]{2,1,0:T(1,128)S(1)}, u32[]{:S(2)}, u32[]{:S(2)}) collective-permute-start(f32[2,1,256]{2,1,0:T(1,128)S(1)} %get-tuple-element.82), channel_id=1, source_target_pairs={{0,8},{8,16},{16,24},{1,9},{9,17},{17,25},{2,10},{10,18},{18,26},{... | collective-permute-start | bytes 6152 | tf_op jit(solution)/shard_map/ppermute | solution.py:29
  25.4 30.5 %collective-permute-start.13 = (f32[2,1,256]{2,1,0:T(1,128)S(1)}, f32[2,1,256]{2,1,0:T(1,128)S(1)}, u32[]{:S(2)}, u32[]{:S(2)}) collective-permute-start(f32[2,1,256]{2,1,0:T(1,128)S(1)} %get-tuple-element.83), channel_id=1, source_target_pairs={{8,0},{16,8},{24,16},{9,1},{17,9},{25,17},{10,2},{18,10},{26,18},{... | collective-permute-start | bytes 6152 | tf_op jit(solution)/shard_map/ppermute | solution.py:32
  26.8 39.8 %collective-permute-start.8 = (f32[3,1,256]{2,1,0:T(1,128)S(1)}, f32[3,1,256]{2,1,0:T(1,128)S(1)}, u32[]{:S(2)}, u32[]{:S(2)}) collective-permute-start(f32[3,1,256]{2,1,0:T(1,128)S(1)} %get-tuple-element.108), channel_id=1, source_target_pairs={{0,8},{8,16},{16,24},{1,9},{9,17},{17,25},{2,10},{10,18},{18,26},{... | collective-permute-start | bytes 9224 | tf_op jit(solution)/shard_map/ppermute | solution.py:29
  31.4 0.7 copy-start.10
  56.0 6.8 %collective-permute-start.14 = (f32[2,34,1]{2,1,0:T(8,128)S(1)}, f32[2,34,1]{2,1,0:T(8,128)S(1)}, u32[]{:S(2)}, u32[]{:S(2)}) collective-permute-start(f32[2,34,1]{2,1,0:T(8,128)S(1)} %get-tuple-element.80), channel_id=1, source_target_pairs={{0,1},{1,2},{2,3},{3,4},{4,5},{5,6},{6,7},{8,9},{9,10},{10,11},{11... | collective-permute-start | bytes 824 | tf_op jit(solution)/shard_map/ppermute | solution.py:29
  60.9 5.5 %collective-permute-start.15 = (f32[2,34,1]{2,1,0:T(8,128)S(1)}, f32[2,34,1]{2,1,0:T(8,128)S(1)}, u32[]{:S(2)}, u32[]{:S(2)}) collective-permute-start(f32[2,34,1]{2,1,0:T(8,128)S(1)} %get-tuple-element.81), channel_id=1, source_target_pairs={{1,0},{2,1},{3,2},{4,3},{5,4},{6,5},{7,6},{9,8},{10,9},{11,10},{12... | collective-permute-start | bytes 824 | tf_op jit(solution)/shard_map/ppermute | solution.py:32
  62.9 5.5 %collective-permute-start.9 = (f32[3,1,256]{2,1,0:T(1,128)S(1)}, f32[3,1,256]{2,1,0:T(1,128)S(1)}, u32[]{:S(2)}, u32[]{:S(2)}) collective-permute-start(f32[3,1,256]{2,1,0:T(1,128)S(1)} %get-tuple-element.109), channel_id=1, source_target_pairs={{8,0},{16,8},{24,16},{9,1},{17,9},{25,17},{10,2},{18,10},{26,18},{... | collective-permute-start | bytes 9224 | tf_op jit(solution)/shard_map/ppermute | solution.py:32
  68.5 6.5 %collective-permute-start.10 = (f32[3,34,1]{2,1,0:T(8,128)S(1)}, f32[3,34,1]{2,1,0:T(8,128)S(1)}, u32[]{:S(2)}, u32[]{:S(2)}) collective-permute-start(f32[3,34,1]{2,1,0:T(8,128)S(1)} %get-tuple-element.68), channel_id=1, source_target_pairs={{0,1},{1,2},{2,3},{3,4},{4,5},{5,6},{6,7},{8,9},{9,10},{10,11},{11... | collective-permute-start | bytes 1232 | tf_op jit(solution)/shard_map/ppermute | solution.py:29
  73.0 5.5 %collective-permute-start.11 = (f32[3,34,1]{2,1,0:T(8,128)S(1)}, f32[3,34,1]{2,1,0:T(8,128)S(1)}, u32[]{:S(2)}, u32[]{:S(2)}) collective-permute-start(f32[3,34,1]{2,1,0:T(8,128)S(1)} %get-tuple-element.69), channel_id=1, source_target_pairs={{1,0},{2,1},{3,2},{4,3},{5,4},{6,5},{7,6},{9,8},{10,9},{11,10},{12... | collective-permute-start | bytes 1232 | tf_op jit(solution)/shard_map/ppermute | solution.py:32
  78.9 5.4 %collective-permute-start.2 = (f32[4,130,1]{2,1,0:T(8,128)S(1)}, f32[4,130,1]{2,1,0:T(8,128)S(1)}, u32[]{:S(2)}, u32[]{:S(2)}) collective-permute-start(f32[4,130,1]{2,1,0:T(8,128)S(1)} %get-tuple-element.28), channel_id=1, source_target_pairs={{0,1},{1,2},{2,3},{3,4},{4,5},{5,6},{6,7},{8,9},{9,10},{10,11},{11... | collective-permute-start | bytes 6248 | tf_op jit(solution)/shard_map/ppermute | solution.py:29
  80.8 7.9 %collective-permute-start.3 = (f32[4,130,1]{2,1,0:T(8,128)S(1)}, f32[4,130,1]{2,1,0:T(8,128)S(1)}, u32[]{:S(2)}, u32[]{:S(2)}) collective-permute-start(f32[4,130,1]{2,1,0:T(8,128)S(1)} %get-tuple-element.29), channel_id=1, source_target_pairs={{1,0},{2,1},{3,2},{4,3},{5,4},{6,5},{7,6},{9,8},{10,9},{11,10},{12... | collective-permute-start | bytes 6248 | tf_op jit(solution)/shard_map/ppermute | solution.py:32
  89.4 0.9 copy-start.2
  90.5 5.9 %collective-permute-start.4 = (f32[4,1,256]{2,1,0:T(1,128)S(1)}, f32[4,1,256]{2,1,0:T(1,128)S(1)}, u32[]{:S(2)}, u32[]{:S(2)}) collective-permute-start(f32[4,1,256]{2,1,0:T(1,128)S(1)} %get-tuple-element.30), channel_id=1, source_target_pairs={{0,8},{8,16},{16,24},{1,9},{9,17},{17,25},{2,10},{10,18},{18,26},{... | collective-permute-start | bytes 12296 | tf_op jit(solution)/shard_map/ppermute | solution.py:29
  95.0 4.4 %collective-permute-start.5 = (f32[4,1,256]{2,1,0:T(1,128)S(1)}, f32[4,1,256]{2,1,0:T(1,128)S(1)}, u32[]{:S(2)}, u32[]{:S(2)}) collective-permute-start(f32[4,1,256]{2,1,0:T(1,128)S(1)} %get-tuple-element.31), channel_id=1, source_target_pairs={{8,0},{16,8},{24,16},{9,1},{17,9},{25,17},{10,2},{18,10},{26,18},{... | collective-permute-start | bytes 12296 | tf_op jit(solution)/shard_map/ppermute | solution.py:32
  99.6 29.0 %collective-permute-start.6 = (f32[4,130,1]{2,1,0:T(8,128)S(1)}, f32[4,130,1]{2,1,0:T(8,128)S(1)}, u32[]{:S(2)}, u32[]{:S(2)}) collective-permute-start(f32[4,130,1]{2,1,0:T(8,128)S(1)} %get-tuple-element.26), channel_id=1, source_target_pairs={{0,1},{1,2},{2,3},{3,4},{4,5},{5,6},{6,7},{8,9},{9,10},{10,11},{11... | collective-permute-start | bytes 6248 | tf_op jit(solution)/shard_map/ppermute | solution.py:29
  102.8 25.8 %collective-permute-start.7 = (f32[4,130,1]{2,1,0:T(8,128)S(1)}, f32[4,130,1]{2,1,0:T(8,128)S(1)}, u32[]{:S(2)}, u32[]{:S(2)}) collective-permute-start(f32[4,130,1]{2,1,0:T(8,128)S(1)} %get-tuple-element.27), channel_id=1, source_target_pairs={{1,0},{2,1},{3,2},{4,3},{5,4},{6,5},{7,6},{9,8},{10,9},{11,10},{12... | collective-permute-start | bytes 6248 | tf_op jit(solution)/shard_map/ppermute | solution.py:32
  129.7 0.7 copy-start.3
  155.0 97.6 %all-reduce.6.cloned.1.call-start = ((), (), s32[]{:S(2)}) async-start(), calls=%async_computation.1 | async-start | bytes 196608 | tf_op jit(solution)/shard_map/psum | solution.py:21
  253.5 4.4 %collective-permute-start.16 = (f32[3,1,256]{2,1,0:T(1,128)S(1)}, f32[3,1,256]{2,1,0:T(1,128)S(1)}, u32[]{:S(2)}, u32[]{:S(2)}) collective-permute-start(f32[3,1,256]{2,1,0:T(1,128)S(1)} %get-tuple-element.78), channel_id=1, source_target_pairs={{0,8},{8,16},{16,24},{1,9},{9,17},{17,25},{2,10},{10,18},{18,26},{... | collective-permute-start | bytes 9224 | tf_op jit(solution)/shard_map/ppermute | solution.py:29
  256.5 4.3 %collective-permute-start.17 = (f32[3,1,256]{2,1,0:T(1,128)S(1)}, f32[3,1,256]{2,1,0:T(1,128)S(1)}, u32[]{:S(2)}, u32[]{:S(2)}) collective-permute-start(f32[3,1,256]{2,1,0:T(1,128)S(1)} %get-tuple-element.79), channel_id=1, source_target_pairs={{8,0},{16,8},{24,16},{9,1},{17,9},{25,17},{10,2},{18,10},{26,18},{... | collective-permute-start | bytes 9224 | tf_op jit(solution)/shard_map/ppermute | solution.py:32
  261.0 7.5 %collective-permute-start.18 = (f32[3,34,1]{2,1,0:T(8,128)S(1)}, f32[3,34,1]{2,1,0:T(8,128)S(1)}, u32[]{:S(2)}, u32[]{:S(2)}) collective-permute-start(f32[3,34,1]{2,1,0:T(8,128)S(1)} %get-tuple-element.64), channel_id=1, source_target_pairs={{0,1},{1,2},{2,3},{3,4},{4,5},{5,6},{6,7},{8,9},{9,10},{10,11},{11... | collective-permute-start | bytes 1232 | tf_op jit(solution)/shard_map/ppermute | solution.py:29
  266.5 5.5 %collective-permute-start.19 = (f32[3,34,1]{2,1,0:T(8,128)S(1)}, f32[3,34,1]{2,1,0:T(8,128)S(1)}, u32[]{:S(2)}, u32[]{:S(2)}) collective-permute-start(f32[3,34,1]{2,1,0:T(8,128)S(1)} %get-tuple-element.65), channel_id=1, source_target_pairs={{1,0},{2,1},{3,2},{4,3},{5,4},{6,5},{7,6},{9,8},{10,9},{11,10},{12... | collective-permute-start | bytes 1232 | tf_op jit(solution)/shard_map/ppermute | solution.py:32
  273.5 5.2 %collective-permute-start.20 = (f32[3,1,256]{2,1,0:T(1,128)S(1)}, f32[3,1,256]{2,1,0:T(1,128)S(1)}, u32[]{:S(2)}, u32[]{:S(2)}) collective-permute-start(f32[3,1,256]{2,1,0:T(1,128)S(1)} %get-tuple-element.76), channel_id=1, source_target_pairs={{0,8},{8,16},{16,24},{1,9},{9,17},{17,25},{2,10},{10,18},{18,26},{... | collective-permute-start | bytes 9224 | tf_op jit(solution)/shard_map/ppermute | solution.py:29
  277.5 4.3 %collective-permute-start.21 = (f32[3,1,256]{2,1,0:T(1,128)S(1)}, f32[3,1,256]{2,1,0:T(1,128)S(1)}, u32[]{:S(2)}, u32[]{:S(2)}) collective-permute-start(f32[3,1,256]{2,1,0:T(1,128)S(1)} %get-tuple-element.77), channel_id=1, source_target_pairs={{8,0},{16,8},{24,16},{9,1},{17,9},{25,17},{10,2},{18,10},{26,18},{... | collective-permute-start | bytes 9224 | tf_op jit(solution)/shard_map/ppermute | solution.py:32
  281.9 5.2 %collective-permute-start.22 = (f32[3,34,1]{2,1,0:T(8,128)S(1)}, f32[3,34,1]{2,1,0:T(8,128)S(1)}, u32[]{:S(2)}, u32[]{:S(2)}) collective-permute-start(f32[3,34,1]{2,1,0:T(8,128)S(1)} %get-tuple-element.62), channel_id=1, source_target_pairs={{0,1},{1,2},{2,3},{3,4},{4,5},{5,6},{6,7},{8,9},{9,10},{10,11},{11... | collective-permute-start | bytes 1232 | tf_op jit(solution)/shard_map/ppermute | solution.py:29
  285.2 5.5 %collective-permute-start.23 = (f32[3,34,1]{2,1,0:T(8,128)S(1)}, f32[3,34,1]{2,1,0:T(8,128)S(1)}, u32[]{:S(2)}, u32[]{:S(2)}) collective-permute-start(f32[3,34,1]{2,1,0:T(8,128)S(1)} %get-tuple-element.63), channel_id=1, source_target_pairs={{1,0},{2,1},{3,2},{4,3},{5,4},{6,5},{7,6},{9,8},{10,9},{11,10},{12... | collective-permute-start | bytes 1232 | tf_op jit(solution)/shard_map/ppermute | solution.py:32
  292.2 3.9 %collective-permute-start.24 = (f32[3,1,256]{2,1,0:T(1,128)S(1)}, f32[3,1,256]{2,1,0:T(1,128)S(1)}, u32[]{:S(2)}, u32[]{:S(2)}) collective-permute-start(f32[3,1,256]{2,1,0:T(1,128)S(1)} %get-tuple-element.74), channel_id=1, source_target_pairs={{0,8},{8,16},{16,24},{1,9},{9,17},{17,25},{2,10},{10,18},{18,26},{... | collective-permute-start | bytes 9224 | tf_op jit(solution)/shard_map/ppermute | solution.py:29
  294.7 4.3 %collective-permute-start.25 = (f32[3,1,256]{2,1,0:T(1,128)S(1)}, f32[3,1,256]{2,1,0:T(1,128)S(1)}, u32[]{:S(2)}, u32[]{:S(2)}) collective-permute-start(f32[3,1,256]{2,1,0:T(1,128)S(1)} %get-tuple-element.75), channel_id=1, source_target_pairs={{8,0},{16,8},{24,16},{9,1},{17,9},{25,17},{10,2},{18,10},{26,18},{... | collective-permute-start | bytes 9224 | tf_op jit(solution)/shard_map/ppermute | solution.py:32
  299.2 5.2 %collective-permute-start.26 = (f32[3,34,1]{2,1,0:T(8,128)S(1)}, f32[3,34,1]{2,1,0:T(8,128)S(1)}, u32[]{:S(2)}, u32[]{:S(2)}) collective-permute-start(f32[3,34,1]{2,1,0:T(8,128)S(1)} %get-tuple-element.60), channel_id=1, source_target_pairs={{0,1},{1,2},{2,3},{3,4},{4,5},{5,6},{6,7},{8,9},{9,10},{10,11},{11... | collective-permute-start | bytes 1232 | tf_op jit(solution)/shard_map/ppermute | solution.py:29
  302.5 5.5 %collective-permute-start.27 = (f32[3,34,1]{2,1,0:T(8,128)S(1)}, f32[3,34,1]{2,1,0:T(8,128)S(1)}, u32[]{:S(2)}, u32[]{:S(2)}) collective-permute-start(f32[3,34,1]{2,1,0:T(8,128)S(1)} %get-tuple-element.61), channel_id=1, source_target_pairs={{1,0},{2,1},{3,2},{4,3},{5,4},{6,5},{7,6},{9,8},{10,9},{11,10},{12... | collective-permute-start | bytes 1232 | tf_op jit(solution)/shard_map/ppermute | solution.py:32
  309.5 3.9 %collective-permute-start.28 = (f32[3,1,256]{2,1,0:T(1,128)S(1)}, f32[3,1,256]{2,1,0:T(1,128)S(1)}, u32[]{:S(2)}, u32[]{:S(2)}) collective-permute-start(f32[3,1,256]{2,1,0:T(1,128)S(1)} %get-tuple-element.72), channel_id=1, source_target_pairs={{0,8},{8,16},{16,24},{1,9},{9,17},{17,25},{2,10},{10,18},{18,26},{... | collective-permute-start | bytes 9224 | tf_op jit(solution)/shard_map/ppermute | solution.py:29
  312.0 4.3 %collective-permute-start.29 = (f32[3,1,256]{2,1,0:T(1,128)S(1)}, f32[3,1,256]{2,1,0:T(1,128)S(1)}, u32[]{:S(2)}, u32[]{:S(2)}) collective-permute-start(f32[3,1,256]{2,1,0:T(1,128)S(1)} %get-tuple-element.73), channel_id=1, source_target_pairs={{8,0},{16,8},{24,16},{9,1},{17,9},{25,17},{10,2},{18,10},{26,18},{... | collective-permute-start | bytes 9224 | tf_op jit(solution)/shard_map/ppermute | solution.py:32
  316.4 5.2 %collective-permute-start.30 = (f32[3,34,1]{2,1,0:T(8,128)S(1)}, f32[3,34,1]{2,1,0:T(8,128)S(1)}, u32[]{:S(2)}, u32[]{:S(2)}) collective-permute-start(f32[3,34,1]{2,1,0:T(8,128)S(1)} %get-tuple-element.58), channel_id=1, source_target_pairs={{0,1},{1,2},{2,3},{3,4},{4,5},{5,6},{6,7},{8,9},{9,10},{10,11},{11... | collective-permute-start | bytes 1232 | tf_op jit(solution)/shard_map/ppermute | solution.py:29
  319.8 5.5 %collective-permute-start.31 = (f32[3,34,1]{2,1,0:T(8,128)S(1)}, f32[3,34,1]{2,1,0:T(8,128)S(1)}, u32[]{:S(2)}, u32[]{:S(2)}) collective-permute-start(f32[3,34,1]{2,1,0:T(8,128)S(1)} %get-tuple-element.59), channel_id=1, source_target_pairs={{1,0},{2,1},{3,2},{4,3},{5,4},{6,5},{7,6},{9,8},{10,9},{11,10},{12... | collective-permute-start | bytes 1232 | tf_op jit(solution)/shard_map/ppermute | solution.py:32
  326.7 3.9 %collective-permute-start.32 = (f32[3,1,256]{2,1,0:T(1,128)S(1)}, f32[3,1,256]{2,1,0:T(1,128)S(1)}, u32[]{:S(2)}, u32[]{:S(2)}) collective-permute-start(f32[3,1,256]{2,1,0:T(1,128)S(1)} %get-tuple-element.70), channel_id=1, source_target_pairs={{0,8},{8,16},{16,24},{1,9},{9,17},{17,25},{2,10},{10,18},{18,26},{... | collective-permute-start | bytes 9224 | tf_op jit(solution)/shard_map/ppermute | solution.py:29
  329.3 4.3 %collective-permute-start.33 = (f32[3,1,256]{2,1,0:T(1,128)S(1)}, f32[3,1,256]{2,1,0:T(1,128)S(1)}, u32[]{:S(2)}, u32[]{:S(2)}) collective-permute-start(f32[3,1,256]{2,1,0:T(1,128)S(1)} %get-tuple-element.71), channel_id=1, source_target_pairs={{8,0},{16,8},{24,16},{9,1},{17,9},{25,17},{10,2},{18,10},{26,18},{... | collective-permute-start | bytes 9224 | tf_op jit(solution)/shard_map/ppermute | solution.py:32
  333.7 5.2 %collective-permute-start.34 = (f32[3,34,1]{2,1,0:T(8,128)S(1)}, f32[3,34,1]{2,1,0:T(8,128)S(1)}, u32[]{:S(2)}, u32[]{:S(2)}) collective-permute-start(f32[3,34,1]{2,1,0:T(8,128)S(1)} %get-tuple-element.56), channel_id=1, source_target_pairs={{0,1},{1,2},{2,3},{3,4},{4,5},{5,6},{6,7},{8,9},{9,10},{10,11},{11... | collective-permute-start | bytes 1232 | tf_op jit(solution)/shard_map/ppermute | solution.py:29
  337.0 5.5 %collective-permute-start.35 = (f32[3,34,1]{2,1,0:T(8,128)S(1)}, f32[3,34,1]{2,1,0:T(8,128)S(1)}, u32[]{:S(2)}, u32[]{:S(2)}) collective-permute-start(f32[3,34,1]{2,1,0:T(8,128)S(1)} %get-tuple-element.57), channel_id=1, source_target_pairs={{1,0},{2,1},{3,2},{4,3},{5,4},{6,5},{7,6},{9,8},{10,9},{11,10},{12... | collective-permute-start | bytes 1232 | tf_op jit(solution)/shard_map/ppermute | solution.py:32
  (1 other events, 0.6 us)
Sparse Core Ops, SparseCore 0:
  155.1 50.5 all-reduce.3
  208.9 43.6 all-reduce.5
